TPU v7x, 128 devices: a whole 4x4x4 slice. The times are simulated.
128 devices in a mesh: ra: 8 (over z, x_lo), dec: 16 (over y, x_hi, core).
Axes of the slice: x: 4 (x_hi: 2, x_lo: 2; x = x_hi * 2 + x_lo), y: 4, z: 4, core: 2. Of those that a mesh axis runs over, the one named last changes fastest.
Arguments:
- forests: bfloat16 [16, 64, 128, 1024], P('ra', 'dec'), may hold values from -6 to 6
- resolution: float32 [16, 64, 128], P('ra', 'dec'), may hold values from 0.3 to 1.2
- pixel_range: int32 [16, 64, 2, 128], P('ra', 'dec'), may hold values from 0 to 1024, as said below
- block_pairs: int32 [8, 16, 40, 3], P('ra', 'dec'), may hold values from -1 to 7, as said below
- block_count: int32 [8, 16], P('ra', 'dec'), may hold values from 10 to 40, as said below
- separation_bin: int32 [8, 16, 40, 128, 128], P('ra', 'dec'), may hold values from 0 to 8
Outputs:
- tile_power: float32 [8, 16, 8, 128], P('ra', 'dec')
- sky_power: float32 [8, 128], replicated
Inputs may be any that keep to these rules, and one draw needn't show every extreme that they name: `pixel_range`: lo < hi for every forest; at least 256 valid pixels. `block_pairs`: each device's list names every one of its own cells once with each of the five offsets (0, 0), (0, 1), (1, -1), (1, 0), (1, 1), in an order drawn from the seed. Slots at or past block_count are ignored. `block_count`: some device has all 40 slots live in every draw.
All inputs are finite; a program needn't handle non-finite values.
Results may differ from a plain program's by a relative error of at most 0.0037.
Values may be sent and summed in bfloat16 or wider, within the bound.
A program may use at most 64 MiB of HBM per device.

v0:
```python
import functools

import jax
import jax.numpy as jnp
from jax import lax
from jax.sharding import Mesh
from jax.sharding import PartitionSpec as P

NSEP = 8
NKB = 128
DEC = ("dec_0", "dec_1", "dec_2")
RA = ("ra_0", "ra_1")
RA_DEC = ("ra_0", "ra_1", "dec_0", "dec_1", "dec_2")


def extended(block, sides, width):
    for axis, dim in sides:
        count = lax.axis_size(axis)
        forward = [(i, i + 1) for i in range(count - 1)]
        backward = [(target, source) for source, target in forward]
        low = lax.ppermute(
            lax.slice_in_dim(block, block.shape[dim] - width, None, axis=dim), axis, forward
        )
        high = lax.ppermute(lax.slice_in_dim(block, 0, width, axis=dim), axis, backward)
        block = jnp.concatenate([low, block, high], axis=dim)
    return block


def from_behind(value, axis, steps):
    count = lax.axis_size(axis)
    leading, last = (max(0, -steps), min(count, count - steps))
    return lax.ppermute(value, axis, [(source, source + steps) for source in range(leading, last)])


def one_axis_at_a_time(x, axes):
    return functools.reduce(lax.psum, axes, x)


def dft_table(length, n_modes):
    sample = jnp.arange(length, dtype=jnp.int32)[:, None]
    mode_index = jnp.arange(n_modes, dtype=jnp.int32)[None, :]
    angles = (sample * mode_index % length).astype(jnp.float32) * (2.0 * jnp.pi / length)
    return jnp.concatenate([jnp.cos(angles), jnp.sin(angles)], axis=1).astype(jnp.bfloat16)


def kbin_table(n_modes, n_bins):
    column = jnp.arange(2 * n_modes, dtype=jnp.int32) % n_modes
    which = column // (n_modes // n_bins)
    return (which[:, None] == jnp.arange(n_bins, dtype=jnp.int32)[None, :]).astype(jnp.float32)


def mask_pixels(flux, pixel_range):
    position = jnp.arange(flux.shape[-1], dtype=jnp.int32)
    lower = pixel_range[..., 0, :][..., None]
    upper = pixel_range[..., 1, :][..., None]
    inside = (position >= lower) & (position < upper)
    return jnp.where(inside, flux, jnp.zeros_like(flux))


def to_spectra(masked, widths, basis):
    length = basis.shape[0]
    n_modes = basis.shape[1] // 2
    raw = jnp.dot(masked, basis, preferred_element_type=jnp.float32)
    wavenum = jnp.arange(n_modes, dtype=jnp.float32) * (2.0 * jnp.pi / length)
    wavenum = jnp.concatenate([wavenum, wavenum])
    window = jnp.exp(-0.5 * (wavenum * widths[..., None]) ** 2)
    return (raw * window).astype(jnp.bfloat16)


def block_term(grid_flat, index_a, index_b, sep_bins):
    n_sep = NSEP
    per_cell = sep_bins.shape[0]
    left = lax.dynamic_index_in_dim(grid_flat, index_a, 0, keepdims=False)
    right = lax.dynamic_index_in_dim(grid_flat, index_b, 0, keepdims=False)
    onehot = (sep_bins[None, :, :] == jnp.arange(n_sep, dtype=jnp.int32)[:, None, None]).astype(
        jnp.bfloat16
    )
    mixed = jnp.dot(
        onehot.reshape(n_sep * per_cell, per_cell), right, preferred_element_type=jnp.float32
    )
    mixed = mixed.reshape(n_sep, per_cell, -1)
    block_sum = jnp.sum(mixed * left.astype(jnp.float32)[None], axis=1)
    pair_counts = jnp.sum(onehot.reshape(n_sep, -1).astype(jnp.float32), axis=1)
    return (block_sum, pair_counts)


def per_device(forests, resolution, pixel_range, block_pairs, block_count, separation_bin):
    cells_ra, cells_dec, per_cell, length = forests.shape
    basis = dft_table(length, length // 2)
    masked = mask_pixels(forests, pixel_range)
    own_spectra = to_spectra(masked, resolution, basis)
    sided = extended(own_spectra, ((DEC, 1),), 1)
    above = from_behind(sided[0:1], RA, -1)
    padded = jnp.concatenate([sided, above], axis=0)
    cols_pad = cells_dec + 2
    grid_flat = padded.reshape(-1, per_cell, length)
    entries = block_pairs[0, 0]
    sep_bins = separation_bin[0, 0]
    live_count = block_count[0, 0]

    def slot_term(slot_index):
        entry_row = entries[slot_index]
        row_a = entry_row[0] // cells_dec
        col_a = entry_row[0] % cells_dec + 1
        index_a = row_a * cols_pad + col_a
        index_b = (row_a + entry_row[1]) * cols_pad + col_a + entry_row[2]
        return block_term(grid_flat, index_a, index_b, sep_bins[slot_index])

    start_value = (jnp.zeros((NSEP, length), jnp.float32), jnp.zeros((NSEP,), jnp.float32))

    def add_masked(slot_index, carry):
        block_sum, counts = slot_term(slot_index)
        is_live = (slot_index < live_count).astype(jnp.float32)
        return (carry[0] + is_live * block_sum, carry[1] + is_live * counts)

    sums, counts = lax.fori_loop(0, entries.shape[0], add_masked, start_value)
    binned = jnp.dot(sums, kbin_table(length // 2, NKB), precision=lax.Precision.HIGHEST)
    tile_power = (binned / (per_cell * length)).reshape(1, 1, NSEP, NKB)
    summed, all_counts = (one_axis_at_a_time(binned, RA_DEC), one_axis_at_a_time(counts, RA_DEC))
    sky_power = summed / jnp.maximum(all_counts, 1.0)[:, None]
    return (tile_power, sky_power)


def solution(mesh):
    split = Mesh(mesh.devices.reshape(4, 2, 4, 2, 2), ("ra_0", "ra_1", "dec_0", "dec_1", "dec_2"))
    placed = (
        P(RA, DEC, None, None),
        P(RA, DEC, None),
        P(RA, DEC, None, None),
        P(RA, DEC, None, None),
        P(RA, DEC),
        P(RA, DEC, None, None, None),
    )
    return jax.shard_map(
        per_device,
        mesh=split,
        in_specs=placed,
        out_specs=(P(RA, DEC, None, None), P()),
        check_vma=False,
    )
```

profile of v0, /device:TPU:1, one launch (start us, length us, event | category | flops | bytes accessed | tf_op | source)
XLA Modules:
  0.0 467.3 jit_solution(17213348893424825261)
XLA Ops:
  0.7 8.5 %sine_convert_fusion = (bf16[1024,512]{1,0:T(8,128)(2,1)S(1)}, bf16[1024,512]{1,0:T(8,128)(2,1)S(1)}) fusion(), kind=kLoop, calls=%fused_computation.32 | loop fusion | flops 8388608 | bytes 2097152 | tf_op jit(solution)/shard_map/convert.2
  9.2 2.9 multiply_convert_fusion
  12.2 6.0 %collective-permute-start = (bf16[2,1,128,1024]{3,2,1,0:T(8,128)(2,1)S(1)}, bf16[2,1,128,1024]{3,2,1,0:T(8,128)(2,1)S(1)}, u32[]{:S(2)}, u32[]{:S(2)}) collective-permute-start(bf16[2,1,128,1024]{3,2,1,0:T(8,128)(2,1)S(1)} %get-tuple-element.237), channel_id=1, source_target_pairs={{0,1},{1,2},{2,3},{3,4},{4,5},{5,6},{6,7},{7,8},{8,9},{9,10},{10,1... | collective-permute-start | bytes 1572872 | tf_op jit(solution)/shard_map/ppermute | solution.py:21
  18.2 1.9 collective-permute-start.1
  20.2 4.2 collective-permute-done
  24.3 7.3 %collective-permute-done.1 = bf16[2,1,128,1024]{3,2,1,0:T(8,128)(2,1)S(1)} collective-permute-done((bf16[2,1,128,1024]{3,2,1,0:T(8,128)(2,1)S(1)}, bf16[2,1,128,1024]{3,2,1,0:T(8,128)(2,1)S(1)}, u32[]{:S(2)}, u32[]{:S(2)}) %collective-permute-start.1) | collective-permute-done | bytes 524320 | tf_op jit(solution)/shard_map/ppermute | solution.py:24
  34.3 27.9 %collective-permute-done.2 = bf16[1,6,128,1024]{3,2,1,0:T(8,128)(2,1)} collective-permute-done((bf16[1,6,128,1024]{3,2,1,0:T(8,128)(2,1)}, bf16[1,6,128,1024]{3,2,1,0:T(8,128)(2,1)}, u32[]{:S(2)}, u32[]{:S(2)}) %collective-permute-start.2) | collective-permute-done | bytes 1572896 | tf_op jit(solution)/shard_map/ppermute | solution.py:32
  62.2 3.6 pad_maximum_fusion
  65.7 356.7 %while.18 = (s32[]{:T(128)}, f32[8,1024]{1,0:T(8,128)S(1)}, f32[8]{0:T(128)S(1)}, s32[]{:T(128)}, s32[40,128,128]{2,1,0:T(8,128)}, /*index=5*/s32[40,3]{0,1:T(4,...) while((s32[]{:T(128)}, f32[8,1024]{1,0:T(8,128)S(1)}, ...), condition=%wide.region_3.4_spmd.clone, body=%wide.region_0.3_spmd.clone.sunk | while | flops 271335488 | bytes 2032321 | solution.py:116
  72.0 1.7 multiply_reduce_fusion.2
  81.0 1.7 multiply_reduce_fusion.2
  89.9 1.7 multiply_reduce_fusion.2
  107.7 1.7 multiply_reduce_fusion.2
  116.6 1.7 multiply_reduce_fusion.2
  125.6 1.7 multiply_reduce_fusion.2
  143.4 1.7 multiply_reduce_fusion.2
  152.3 1.7 multiply_reduce_fusion.2
  161.2 1.7 multiply_reduce_fusion.2
  170.1 1.7 multiply_reduce_fusion.2
  179.1 1.7 multiply_reduce_fusion.2
  188.0 1.7 multiply_reduce_fusion.2
  196.9 1.7 multiply_reduce_fusion.2
  205.8 1.7 multiply_reduce_fusion.2
  214.7 1.7 multiply_reduce_fusion.2
  223.7 1.7 multiply_reduce_fusion.2
  232.6 1.7 multiply_reduce_fusion.2
  241.5 1.7 multiply_reduce_fusion.2
  250.4 1.7 multiply_reduce_fusion.2
  259.3 1.7 multiply_reduce_fusion.2
  277.2 1.7 multiply_reduce_fusion.2
  286.1 1.7 multiply_reduce_fusion.2
  295.0 1.7 multiply_reduce_fusion.2
  312.8 1.7 multiply_reduce_fusion.2
  321.8 1.7 multiply_reduce_fusion.2
  330.7 1.7 multiply_reduce_fusion.2
  339.6 1.7 multiply_reduce_fusion.2
  348.5 1.7 multiply_reduce_fusion.2
  357.4 1.7 multiply_reduce_fusion.2
  366.3 1.7 multiply_reduce_fusion.2
  375.3 1.7 multiply_reduce_fusion.2
  384.2 1.7 multiply_reduce_fusion.2
  393.1 1.7 multiply_reduce_fusion.2
  402.0 1.7 multiply_reduce_fusion.2
  423.4 10.0 %all-reduce.1 = (f32[8,128]{1,0:T(8,128)S(1)}, f32[8]{0:T(128)S(1)}) all-reduce(f32[8,128]{1,0:T(8,128)S(1)} %fusion.22, f32[8]{0:T(128)S(1)} %get-tuple-element.183), channel_id=1, replica_groups=mesh['ra_0'=4,'ra_1'=2,'dec_0'=4,'dec_1'=2,'dec_2'=2] {'ra_0'}, use_global_device_ids=true, to_apply=%region_4.5 | all-reduce | flops 1032 | bytes 8256 | tf_op jit(solution)/shard_map/psum | solution.py:36
  433.4 3.9 all-reduce.4
  437.3 16.9 %all-reduce = (f32[8,128]{1,0:T(8,128)S(1)}, f32[8]{0:T(128)S(1)}) all-reduce(f32[8,128]{1,0:T(8,128)S(1)} %get-tuple-element.230, f32[8]{0:T(128)S(1)} %get-tuple-element.231), channel_id=1, replica_groups=mesh['ra_0'=4,'ra_1'=2,'dec_0'=4,'dec_1'=2,'dec_2'=2] {'dec_0'}, use_global_device_ids=true, to_apply=%region_6.7 | all-reduce | flops 1032 | bytes 8256 | tf_op jit(solution)/shard_map/psum | solution.py:36
  454.2 5.4 %all-reduce.3 = (f32[8,128]{1,0:T(8,128)S(1)}, f32[8]{0:T(128)S(1)}) all-reduce(f32[8,128]{1,0:T(8,128)S(1)} %get-tuple-element.222, f32[8]{0:T(128)S(1)} %get-tuple-element.223), channel_id=1, replica_groups=mesh['ra_0'=4,'ra_1'=2,'dec_0'=4,'dec_1'=2,'dec_2'=2] {'dec_1'}, use_global_device_ids=true, to_apply=%region_7.8 | all-reduce | flops 1032 | bytes 8256 | tf_op jit(solution)/shard_map/psum | solution.py:36
  459.6 7.1 %all-reduce.2 = (f32[8,128]{1,0:T(8,128)S(1)}, f32[8]{0:T(128)S(1)}) all-reduce(f32[8,128]{1,0:T(8,128)S(1)} %get-tuple-element.228, f32[8]{0:T(128)S(1)} %get-tuple-element.229), channel_id=1, replica_groups=mesh['ra_0'=4,'ra_1'=2,'dec_0'=4,'dec_1'=2,'dec_2'=2] {'dec_2'}, use_global_device_ids=true, to_apply=%region_8.9 | all-reduce | flops 1032 | bytes 8256 | tf_op jit(solution)/shard_map/psum | solution.py:36
  (308 shorter events, 125.9 us)
Async XLA Ops:
  0.6 8.5 %copy-start = (s32[2,4,2,128]{3,2,1,0:T(2,128)S(1)}, s32[2,4,2,128]{3,2,1,0:T(2,128)}, u32[]{:S(2)}) copy-start(s32[2,4,2,128]{3,2,1,0:T(2,128)} %param.10) | copy-start | bytes 24580
  0.6 8.6 %copy-start.2 = (bf16[2,4,128,1024]{3,2,1,0:T(8,128)(2,1)S(1)}, bf16[2,4,128,1024]{3,2,1,0:T(8,128)(2,1)}, u32[]{:S(2)}) copy-start(bf16[2,4,128,1024]{3,2,1,0:T(8,128)(2,1)} %param.8) | copy-start | bytes 6291460
  0.6 8.6 %copy-start.3 = (f32[2,4,128]{2,1,0:T(4,128)S(1)}, f32[2,4,128]{2,1,0:T(4,128)}, u32[]{:S(2)}) copy-start(f32[2,4,128]{2,1,0:T(4,128)} %param.9) | copy-start | bytes 12292
  12.2 12.1 %collective-permute-start = (bf16[2,1,128,1024]{3,2,1,0:T(8,128)(2,1)S(1)}, bf16[2,1,128,1024]{3,2,1,0:T(8,128)(2,1)S(1)}, u32[]{:S(2)}, u32[]{:S(2)}) collective-permute-start(bf16[2,1,128,1024]{3,2,1,0:T(8,128)(2,1)S(1)} %get-tuple-element.237), channel_id=1, source_target_pairs={{0,1},{1,2},{2,3},{3,4},{4,5},{5,6},{6,7},{7,8},{8,9},{9,10},{10,1... | collective-permute-start | bytes 1572872 | tf_op jit(solution)/shard_map/ppermute | solution.py:21
  18.2 16.1 %copy-start.1 = (s32[1,1,40,3]{2,1,3,0:T(1,128)S(1)}, s32[1,1,40,3]{2,1,3,0:T(1,128)}, u32[]{:S(2)}) copy-start(s32[1,1,40,3]{2,1,3,0:T(1,128)} %param.11) | copy-start | bytes 1444
  18.2 13.4 %collective-permute-start.1 = (bf16[2,1,128,1024]{3,2,1,0:T(8,128)(2,1)S(1)}, bf16[2,1,128,1024]{3,2,1,0:T(8,128)(2,1)S(1)}, u32[]{:S(2)}, u32[]{:S(2)}) collective-permute-start(bf16[2,1,128,1024]{3,2,1,0:T(8,128)(2,1)S(1)} %get-tuple-element.238), channel_id=1, source_target_pairs={{1,0},{2,1},{3,2},{4,3},{5,4},{6,5},{7,6},{8,7},{9,8},{10,9},{11,1... | collective-permute-start | bytes 1572872 | tf_op jit(solution)/shard_map/ppermute | solution.py:24
  33.0 29.2 %collective-permute-start.2 = (bf16[1,6,128,1024]{3,2,1,0:T(8,128)(2,1)}, bf16[1,6,128,1024]{3,2,1,0:T(8,128)(2,1)}, u32[]{:S(2)}, u32[]{:S(2)}) collective-permute-start(bf16[1,6,128,1024]{3,2,1,0:T(8,128)(2,1)} %pad_maximum_fusion.1), channel_id=1, source_target_pairs={{16,0},{32,16},{48,32},{64,48},{80,64},{96,80},{112,96},{17,1},{33... | collective-permute-start | bytes 4718600 | tf_op jit(solution)/shard_map/ppermute | solution.py:32
where the time goes:
time: 474 us; the launch traced here: 467 us
  loops' own time  179 us (38%)
  matrix products  69.8 us (15%)
  other arithmetic  65.4 us (14%)
  local copies, waits for them, and re-layouts  60.9 us (13%)
  blocking collectives  43.2 us (9%)
  waiting for transfers between devices  39.3 us (8%)
  starting transfers between devices  9.23 us (2%)
    another operation x1, loops' own time, per_device(): sums, counts = lax.fori_loop(0, entries.shape[0], add_masked, start_value)  179 us
    dot_general x40, matrix products, block_term(): jnp.dot(onehot.reshape(n_sep * per_cell, per_cell), right, preferred_elem...  66.5 us
    psum x5, blocking collectives, one_axis_at_a_time(): return functools.reduce(lax.psum, axes, x)  43.2 us
    mul x40, other arithmetic, block_term(): block_sum = jnp.sum(mixed * left.astype(jnp.float32)[None], axis=1)  39.8 us
    eq x40, local copies, waits for them, and re-layouts, block_term(): sep_bins[None, :, :] == jnp.arange(n_sep, dtype=jnp.int32)[:, None, None]  34.2 us
    ppermute x1, waiting for transfers between devices, from_behind(): lax.ppermute(value, axis, [(source, source + steps) for source in range(l...  27.9 us
    slice x40, local copies, waits for them, and re-layouts, slot_term(): index_b = (row_a + entry_row[1]) * cols_pad + col_a + entry_row[2]  23.6 us
    reduce_sum x40, other arithmetic, block_term(): pair_counts = jnp.sum(onehot.reshape(n_sep, -1).astype(jnp.float32), axis=1)  9.94 us
  transfers between devices with their start and end apart: 3, of which 3 were waited for; matrix products, arithmetic and copies ran while one was open for 0% of the time, Pallas kernels for 0%

commit v1 on v0

v1 whole, which is shorter than its diff:
```python
import functools

import jax
import jax.numpy as jnp
import ml_dtypes
import numpy as np
from jax import lax
from jax.experimental import pallas as pl
from jax.experimental.pallas import tpu as pltpu
from jax.sharding import PartitionSpec as P

MESH = pl.DeviceIdType.MESH
NSEP = 8
NKB = 128
FPC = 128
NPIX = 1024
MODES = NPIX // 2
STRIDE = 6
TILE = 256
F32 = jnp.float32
BF16 = jnp.bfloat16


def dft_table():
    sample = np.arange(NPIX, dtype=np.int64)[:, None]
    mode = np.arange(MODES, dtype=np.int64)[None, :]
    angles = (sample * mode % NPIX).astype(np.float64) * (2.0 * np.pi / NPIX)
    table = np.concatenate([np.cos(angles), np.sin(angles)], axis=1)
    return table.astype(np.float32).astype(ml_dtypes.bfloat16)


def at(row, col):
    return row * STRIDE + col + 1


def kernel(
    n_ra, n_dec,
    forests, resolution, pixel_range, pairs, count, sep_hbm, basis_hbm,
    tile_out, sky_out,
    flux, basis, sep, spec, masked, onehot, acc, cacc, inv_v, inv_s, pay, pay2, box1, box2,
    load_sem, halo_sem, send_sem, sent1, got1, sent2, got2,
):
    p = lax.axis_index("ra")
    q = lax.axis_index("dec")
    odd = lax.rem(q, 2) == 1
    even = jnp.logical_not(odd)
    above, below = p < n_ra - 1, p > 0
    right, left = q < n_dec - 1, q > 0

    loads = [pltpu.make_async_copy(basis_hbm, basis, load_sem.at[0])]
    for k in range(4):
        cells = pl.ds(2 * (k % 2), 2)
        loads.append(pltpu.make_async_copy(
            forests.at[k // 2, cells], flux.at[pl.ds(2 * k, 2)], load_sem.at[1 + k]))
    loads.append(pltpu.make_async_copy(sep_hbm.at[0, 0], sep, load_sem.at[5]))
    loads[1].start()
    loads[0].start()
    for load in loads[2:]:
        load.start()

    barrier = pltpu.get_barrier_semaphore()
    for k in range(1, n_dec):
        pl.semaphore_signal(barrier, inc=1, device_id=(p, lax.rem(q + k, n_dec)), device_id_type=MESH)
    for k in range(1, n_ra):
        pl.semaphore_signal(barrier, inc=1, device_id=(lax.rem(p + k, n_ra), q), device_id_type=MESH)
    expected = jnp.int32(n_dec + n_ra - 2)
    for ok, dp, dq in (
        (above & right, 1, 1), (above & left, 1, -1), (below & right, -1, 1), (below & left, -1, -1),
    ):
        @pl.when(ok)
        def _():
            pl.semaphore_signal(barrier, inc=1, device_id=(p + dp, q + dq), device_id_type=MESH)
        expected += ok.astype(jnp.int32)

    entry = pairs[0, 0]
    step = jnp.where(entry[:, 1:2] == 0, entry[:, 2:3], entry[:, 2:3] + 3)
    code = entry[:, 0:1] * 5 + step
    slots = code.shape[0]
    hit = code == lax.broadcasted_iota(jnp.int32, (slots, 128), 1)
    slot_id = lax.broadcasted_iota(jnp.int32, (slots, 128), 0)
    inverse = jnp.max(jnp.where(hit, slot_id, 0), axis=0, keepdims=True)
    inv_v[...] = jnp.broadcast_to(inverse, inv_v.shape)
    to_smem = pltpu.make_async_copy(inv_v, inv_s, load_sem.at[6])
    to_smem.start()
    live_count = count[0, 0]

    blank = jnp.zeros((FPC, NPIX), BF16)
    for gone, cells in (
        (jnp.logical_not(above), [at(2, c) for c in range(-1, 5)]),
        (jnp.logical_not(right), [at(0, 4), at(1, 4), at(2, 4)]),
        (jnp.logical_not(left), [at(1, -1), at(2, -1)]),
    ):
        @pl.when(gone)
        def _():
            for cell in cells:
                spec[cell] = blank
    acc[...] = jnp.zeros_like(acc)
    cacc[...] = jnp.zeros_like(cacc)

    def send(source, target, sem, dp, dq):
        return pltpu.make_async_remote_copy(
            src_ref=spec.at[source], dst_ref=spec.at[target],
            send_sem=send_sem.at[sem], recv_sem=halo_sem.at[target],
            device_id=(p + dp, q + dq), device_id_type=MESH)

    def arrived(target):
        send(target, target, 0, 0, 0).wait_recv()

    down = [(send(at(0, c), at(2, c), c, -1, 0), below) for c in range(4)]
    down_left = (send(at(0, 0), at(2, 4), 4, -1, -1), below & left & even)
    down_right = (send(at(0, 3), at(2, -1), 5, -1, 1), below & right & odd)
    side = [
        (send(at(0, 0), at(0, 4), 6, 0, -1), left),
        (send(at(1, 0), at(1, 4), 7, 0, -1), left),
        (send(at(1, 3), at(1, -1), 8, 0, 1), right),
    ]
    pass_left = (send(at(2, 0), at(2, 4), 9, 0, -1), above & odd)
    pass_right = (send(at(2, 3), at(2, -1), 10, 0, 1), above & even)

    def start(entry):
        copy, ok = entry

        @pl.when(ok)
        def _():
            copy.start()

    widths = jnp.transpose(jnp.concatenate([resolution[0], resolution[1]], axis=0))
    bounds = [pixel_range[r, c] for r in range(2) for c in range(4)]
    bounds = jnp.transpose(jnp.concatenate(bounds, axis=0))
    position = lax.broadcasted_iota(jnp.int32, (FPC, NPIX), 1)
    wave = lax.broadcasted_iota(jnp.int32, (1, MODES), 1).astype(F32) * (2.0 * np.pi / NPIX)

    def spectra(k):
        loads[1 + k].wait()
        windows = []
        for h in range(2):
            cell = 2 * k + h
            low, high = bounds[:, 2 * cell:2 * cell + 1], bounds[:, 2 * cell + 1:2 * cell + 2]
            inside = (position >= low) & (position < high)
            masked[pl.ds(h * FPC, FPC)] = jnp.where(inside, flux[cell].astype(F32), 0.0).astype(BF16)
            windows.append(jnp.exp(-0.5 * (wave * widths[:, cell:cell + 1]) ** 2))
        if k == 0:
            loads[0].wait()
        for n in range(NPIX // TILE):
            cols = pl.ds(n * TILE, TILE)
            raw = jnp.dot(masked[...], basis[:, cols], preferred_element_type=F32)
            first = n * TILE % MODES
            for h in range(2):
                cell = at(k // 2, 2 * (k % 2) + h)
                value = raw[h * FPC:(h + 1) * FPC] * windows[h][:, first:first + TILE]
                spec[cell, :, cols] = value.astype(BF16)

    spectra(0)
    pl.semaphore_wait(barrier, expected)
    for entry in (down[0], down[1], down_left, side[0]):
        start(entry)
    spectra(1)
    for entry in (down[3], down[2], down_right):
        start(entry)
    spectra(2)
    start(side[1])
    spectra(3)
    start(side[2])

    loads[5].wait()
    to_smem.wait()

    def pair_up(a, b, first_code, n):
        for k in range(n):
            slot = inv_s[0, first_code + k]
            dead = jnp.where(slot < live_count, 0, 16)
            which = (sep[slot] + dead).astype(F32).astype(BF16)
            for t in range(NSEP):
                ones = jnp.where(which == jnp.asarray(t, BF16), jnp.asarray(1, BF16), jnp.asarray(0, BF16))
                onehot[pl.ds(t * FPC, FPC), pl.ds(k * FPC, FPC)] = ones
                cacc[t] += jnp.sum(ones.astype(F32).reshape(16, 8, FPC), axis=0)
        for m in range(NPIX // TILE):
            cols = pl.ds(m * TILE, TILE)
            partner = spec[pl.ds(b, n), :, cols].reshape(n * FPC, TILE)
            own = spec[a, :, cols].astype(F32).reshape(1, 16, 8, TILE)
            mixed = jnp.dot(onehot[:, :n * FPC], partner, preferred_element_type=F32)
            acc[:, :, cols] += jnp.sum(mixed.reshape(NSEP, 16, 8, TILE) * own, axis=1)

    def code_of(row, col, offset):
        return (row * 4 + col) * 5 + offset

    @pl.loop(0, 6)
    def _(k):
        row, col = k // 3, k % 3
        pair_up(at(row, col), at(row, col), code_of(row, col, 0), 2)

    @pl.loop(1, 3)
    def _(col):
        pair_up(at(0, col), at(1, col - 1), code_of(0, col, 2), 3)

    @pl.loop(0, 2)
    def _(k):
        col = 3 * k
        pair_up(at(0, col), at(1, col - k), code_of(0, col, 3 - k), 2)

    @pl.loop(0, 2)
    def _(row):
        pair_up(at(row, 3), at(row, 3), code_of(row, 3, 0), 1)

    for entry, cell in ((pass_left, at(2, 0)), (pass_right, at(2, 3))):
        @pl.when(entry[1])
        def _():
            arrived(cell)
            entry[0].start()

    for ok, cell in ((right, at(0, 4)), (right, at(1, 4)), (left, at(1, -1))):
        @pl.when(ok)
        def _():
            arrived(cell)

    @pl.loop(0, 2)
    def _(row):
        pair_up(at(row, 3), at(row, 4), code_of(row, 3, 1), 1)

    @pl.loop(0, 2)
    def _(k):
        col = 3 * k
        pair_up(at(0, col), at(1, col - 1 + 2 * k), code_of(0, col, 2 + 2 * k), 1)

    for ok, cell in (
        (above & even, at(2, 0)), (above, at(2, 1)), (above, at(2, 2)), (above & odd, at(2, 3)),
        (above & left, at(2, -1)), (above & right, at(2, 4)),
    ):
        @pl.when(ok)
        def _():
            arrived(cell)

    @pl.loop(0, 4)
    def _(col):
        pair_up(at(1, col), at(2, col - 1), code_of(1, col, 2), 3)

    column = lax.broadcasted_iota(jnp.int32, (NPIX, NKB), 0) % MODES
    which = column // (MODES // NKB) == lax.broadcasted_iota(jnp.int32, (NPIX, NKB), 1)
    table = jnp.where(which, 1.0, 0.0).astype(BF16)
    rest = acc[...].reshape(NSEP * 8, NPIX)
    folded = jnp.zeros((NSEP * 8, NKB), F32)
    for _ in range(3):
        part = rest.astype(BF16)
        folded += jnp.dot(part, table, preferred_element_type=F32)
        rest = rest - part.astype(F32)
    binned = jnp.sum(folded.reshape(NSEP, 8, NKB), axis=1)
    tile_out[0, 0] = binned * (1.0 / (FPC * NPIX))
    pay[0] = binned
    pay[1] = jnp.sum(cacc[...], axis=1)

    def everyone(source, box, mine, size, sent, got, peer):
        box[mine] = source[...]

        def copy(k):
            return pltpu.make_async_remote_copy(
                src_ref=source, dst_ref=box.at[mine], send_sem=sent.at[k], recv_sem=got.at[mine],
                device_id=peer(lax.rem(mine + k, size)), device_id_type=MESH)

        for k in range(1, size):
            copy(k).start()
        for k in range(1, size):
            other = lax.rem(mine + k, size)
            pltpu.make_async_remote_copy(
                src_ref=source, dst_ref=box.at[other], send_sem=sent.at[k], recv_sem=got.at[other],
                device_id=peer(other), device_id_type=MESH).wait_recv()
        total = box[0]
        for k in range(1, size):
            total = total + box[k]
        return total, [copy(k) for k in range(1, size)]

    total, first = everyone(pay, box1, q, n_dec, sent1, got1, lambda k: (p, k))
    pay2[...] = total
    total, second = everyone(pay2, box2, p, n_ra, sent2, got2, lambda k: (k, q))
    counts = jnp.sum(total[1], axis=1, keepdims=True)
    sky_out[...] = total[0] / jnp.maximum(counts, 1.0)

    for copy in first + second:
        copy.wait_send()
    for copy, ok in down + side + [down_left, down_right, pass_left, pass_right]:
        @pl.when(ok)
        def _():
            copy.wait_send()


def per_device(n_ra, n_dec, forests, resolution, pixel_range, pairs, count, sep):
    vmem = pl.BlockSpec(memory_space=pltpu.VMEM)
    smem = pl.BlockSpec(memory_space=pltpu.SMEM)
    anywhere = pl.BlockSpec(memory_space=pl.ANY)
    dma = pltpu.SemaphoreType.DMA
    return pl.pallas_call(
        functools.partial(kernel, n_ra, n_dec),
        out_shape=(
            jax.ShapeDtypeStruct((1, 1, NSEP, NKB), F32),
            jax.ShapeDtypeStruct((NSEP, NKB), F32),
        ),
        in_specs=[anywhere, vmem, vmem, vmem, smem, anywhere, anywhere],
        out_specs=(vmem, vmem),
        scratch_shapes=[
            pltpu.VMEM((8, FPC, NPIX), BF16),
            pltpu.VMEM((NPIX, NPIX), BF16),
            pltpu.VMEM(sep.shape[2:], jnp.int32),
            pltpu.VMEM((3 * STRIDE, FPC, NPIX), BF16),
            pltpu.VMEM((2 * FPC, NPIX), BF16),
            pltpu.VMEM((NSEP * FPC, 3 * FPC), BF16),
            pltpu.VMEM((NSEP, 8, NPIX), F32),
            pltpu.VMEM((NSEP, 8, FPC), F32),
            pltpu.VMEM((8, 128), jnp.int32),
            pltpu.SMEM((8, 128), jnp.int32),
            pltpu.VMEM((2, NSEP, NKB), F32),
            pltpu.VMEM((2, NSEP, NKB), F32),
            pltpu.VMEM((n_dec, 2, NSEP, NKB), F32),
            pltpu.VMEM((n_ra, 2, NSEP, NKB), F32),
            dma((7,)),
            dma((3 * STRIDE,)),
            dma((11,)),
            dma((n_dec,)),
            dma((n_dec,)),
            dma((n_ra,)),
            dma((n_ra,)),
        ],
        compiler_params=pltpu.CompilerParams(
            collective_id=0, has_side_effects=True, vmem_limit_bytes=56 * 1024 * 1024
        ),
        cost_estimate=pl.CostEstimate(flops=13_000_000_000, bytes_accessed=7_000_000, transcendentals=500_000),
    )(forests, resolution, pixel_range, pairs, count, sep, jnp.asarray(dft_table()))


def solution(mesh):
    n_ra, n_dec = mesh.shape["ra"], mesh.shape["dec"]
    return jax.shard_map(
        functools.partial(per_device, n_ra, n_dec),
        mesh=mesh,
        in_specs=(
            P("ra", "dec", None, None),
            P("ra", "dec", None),
            P("ra", "dec", None, None),
            P("ra", "dec", None, None),
            P("ra", "dec"),
            P("ra", "dec", None, None, None),
        ),
        out_specs=(P("ra", "dec", None, None), P()),
        check_vma=False,
    )
```

time: 474 us -> 70.9 us (0.15); the launches traced: 467 us -> 70.6 us
  loops' own time: 179 us -> 0 us
  matrix products: 69.8 us -> 0 us
  Pallas kernels: 0 us -> 65.4 us
  other arithmetic: 65.4 us -> 0 us
  local copies, waits for them, and re-layouts: 60.9 us -> 3.91 us
  blocking collectives: 43.2 us -> 0 us
  waiting for transfers between devices: 39.3 us -> 0 us
  starting transfers between devices: 9.23 us -> 0 us
    another operation x1 -> x0, loops' own time: 179 us -> none  [per_device(): sums, counts = lax.fori_loop(0, entries.shape[0], add_masked, start_value)]
    dot_general x42 -> x0, matrix products: 69.8 us -> none  [the longest x40 66.5 us: block_term(): jnp.dot(onehot.reshape(n_sep * per_cell, per_cell), right, preferred_elem...]
    pallas_call x0 -> x1, Pallas kernels: none -> 65.4 us  [per_device(): pl.pallas_call(functools.partial(kernel, n_ra, n_dec), out_shape=(jax.Sha...]
    psum x5 -> x0, blocking collectives: 43.2 us -> none  [one_axis_at_a_time(): return functools.reduce(lax.psum, axes, x)]
    mul x41 -> x0, other arithmetic: 39.8 us -> none  [the longest x40 39.8 us: block_term(): block_sum = jnp.sum(mixed * left.astype(jnp.float32)[None], axis=1)]
    ppermute x3 -> x0, waiting for transfers between devices: 39.3 us -> none  [the longest x1 27.9 us: from_behind(): lax.ppermute(value, axis, [(source, source + steps) for source in range(l...]
    eq x40 -> x0, local copies, waits for them, and re-layouts: 34.2 us -> none  [block_term(): sep_bins[None, :, :] == jnp.arange(n_sep, dtype=jnp.int32)[:, None, None]]
    slice x42 -> x0, local copies, waits for them, and re-layouts: 23.7 us -> none  [the longest x40 23.6 us: slot_term(): index_b = (row_a + entry_row[1]) * cols_pad + col_a + entry_row[2]]
  transfers between devices with their start and end apart: 3 -> 0, of which waited for: 3 -> 0; matrix products, arithmetic and copies ran while one was open for 0% -> 0% of each run, Pallas kernels for 0% -> 0%
where the time goes in v1:
time: 70.9 us; the launch traced here: 70.6 us
  Pallas kernels  65.4 us (92%)
  local copies, waits for them, and re-layouts  3.91 us (6%)
  between operations  1.29 us (2%)
    pallas_call x1, Pallas kernels, per_device(): pl.pallas_call(functools.partial(kernel, n_ra, n_dec), out_shape=(jax.Sha...  65.4 us
    unnamed x3, local copies, waits for them, and re-layouts  3.91 us

profile of v1, /device:TPU:1, one launch (start us, length us, event | category | flops | bytes accessed | tf_op | source)
XLA Modules:
  0.0 70.6 jit_solution(8976809346868195523)
XLA Ops:
  1.3 1.4 %copy.9.pairs = s32[1,1,40,3]{3,2,1,0:T(8,128)} copy(s32[1,1,40,3]{2,1,3,0:T(1,128)} %param.10) | data formatting | bytes 960 | tf_op args[3]
  2.6 65.4 %shard_map.86 = (f32[1,1,8,128]{3,2,1,0:T(8,128)}, f32[8,128]{1,0:T(8,128)}) custom-call(bf16[2,4,128,1024]{3,2,1,0:T(8,128)(2,1)} %forests.1, f32[2,4,128]{2,1,0:T(4,128)} %resolution.1, s32[2,4,2,128]{3,2,1,0:T(2,128)} %pixel_range.1, s32[1,1,40,3]{3,2,1,0:T(8,128)} %copy.9.pairs, s32[1,1]{1,0:T(1,128)S(6)} %copy.12.count, ...), custom_call_target="tpu_custom_call" | custom-call | flops 12999999488 | bytes 7000000 | tf_op jit(solution)/shard_map/pallas_call | solution.py:290
  68.1 1.3 %copy.13 = f32[1,1,8,128]{3,2,1,0:T(8,128)} copy(f32[1,1,8,128]{3,2,1,0:T(8,128)} %get-tuple-element.4) | data formatting | bytes 8192
  69.4 1.3 %copy.14 = f32[8,128]{1,0:T(8,128)} copy(f32[8,128]{1,0:T(8,128)} %get-tuple-element.5) | data formatting | bytes 8192

commit v2 on v1

v2 whole, which is shorter than its diff:
```python
import functools

import jax
import jax.numpy as jnp
import ml_dtypes
import numpy as np
from jax import lax
from jax.experimental import pallas as pl
from jax.experimental.pallas import tpu as pltpu
from jax.sharding import PartitionSpec as P

MESH = pl.DeviceIdType.MESH
NSEP = 8
NKB = 128
FPC = 128
NPIX = 1024
MODES = NPIX // 2
STRIDE = 6
TILE = 256
F32 = jnp.float32
BF16 = jnp.bfloat16


def dft_table():
    sample = np.arange(NPIX, dtype=np.int64)[:, None]
    mode = np.arange(MODES, dtype=np.int64)[None, :]
    angles = (sample * mode % NPIX).astype(np.float64) * (2.0 * np.pi / NPIX)
    table = np.concatenate([np.cos(angles), np.sin(angles)], axis=1)
    return table.astype(np.float32).astype(ml_dtypes.bfloat16)


def at(row, col):
    return row * STRIDE + col + 1


def kernel(
    n_ra, n_dec,
    forests, resolution, pixel_range, pairs, count, sep_hbm, basis_hbm,
    out,
    flux, basis, sep, spec, masked, onehot, acc, acc2, cacc, inv_v, inv_s, ship, shipped, lent, lent_in,
    pay, pay2, box1, box2, widths_v, range_v, pairs_v,
    load_sem, halo_sem, send_sem, sent1, got1, sent2, got2,
):
    p = lax.axis_index("ra")
    q = lax.axis_index("dec")
    odd = lax.rem(q, 2) == 1
    even = jnp.logical_not(odd)
    above, below = p < n_ra - 1, p > 0
    right, left = q < n_dec - 1, q > 0

    def load(source, target, k):
        return pltpu.make_async_copy(source, target, load_sem.at[k])

    flux_loads = [load(forests.at[k // 4, k % 4], flux.at[k], k) for k in range(8)]
    basis_load = load(basis_hbm, basis, 8)
    sep_load = load(sep_hbm.at[0, 0], sep, 9)
    small = [load(resolution, widths_v, 10), load(pixel_range, range_v, 11), load(pairs, pairs_v, 12)]
    to_smem = load(inv_v, inv_s, 13)
    for each in small[:2] + [flux_loads[0], flux_loads[3], basis_load, small[2]]:
        each.start()
    for k in (1, 2, 4, 7, 5, 6):
        flux_loads[k].start()
    sep_load.start()

    barrier = pltpu.get_barrier_semaphore()
    expected = jnp.int32(n_dec + n_ra - 2)
    for ok, dp, dq in (
        (above & right, 1, 1), (above & left, 1, -1), (below & right, -1, 1), (below & left, -1, -1),
    ):
        @pl.when(ok)
        def _():
            pl.semaphore_signal(barrier, inc=1, device_id=(p + dp, q + dq), device_id_type=MESH)
        expected += ok.astype(jnp.int32)
    for k in range(1, n_ra):
        pl.semaphore_signal(barrier, inc=1, device_id=(lax.rem(p + k, n_ra), q), device_id_type=MESH)
    for k in range(1, n_dec):
        pl.semaphore_signal(barrier, inc=1, device_id=(p, lax.rem(q + k, n_dec)), device_id_type=MESH)

    def send(source, target, sem, dp, dq):
        return pltpu.make_async_remote_copy(
            src_ref=spec.at[source], dst_ref=spec.at[target],
            send_sem=send_sem.at[sem], recv_sem=halo_sem.at[target],
            device_id=(p + dp, q + dq), device_id_type=MESH)

    def arrived(target, ok):
        @pl.when(ok)
        def _():
            send(target, target, 0, 0, 0).wait_recv()

    bins_there = 3 * STRIDE
    sums_back = bins_there + 1
    down = [(send(at(0, c), at(2, c), c, -1, 0), below) for c in range(4)]
    down_left = (send(at(0, 0), at(2, 4), 4, -1, -1), below & left & even)
    side_low = (send(at(0, 0), at(0, 4), 5, 0, -1), odd | (left & jnp.logical_not(below)))
    side_high = (send(at(1, 0), at(1, 4), 6, 0, -1), left)
    side_right = (send(at(1, 3), at(1, -1), 7, 0, 1), even)
    pass_left = (send(at(2, 0), at(2, 4), 8, 0, -1), above & odd)
    pass_right = (send(at(2, 3), at(2, -1), 9, 0, 1), above & even)
    pass_up = (send(at(2, 0), at(0, 4), 10, 1, -1), above & left & even)
    lend_bins = (pltpu.make_async_remote_copy(
        src_ref=ship, dst_ref=shipped, send_sem=send_sem.at[11], recv_sem=halo_sem.at[bins_there],
        device_id=(p, q - 1), device_id_type=MESH), even & left)
    give_back = (pltpu.make_async_remote_copy(
        src_ref=lent, dst_ref=lent_in, send_sem=send_sem.at[12], recv_sem=halo_sem.at[sums_back],
        device_id=(p, q + 1), device_id_type=MESH), odd & right)

    def start(entry):
        copy, ok = entry

        @pl.when(ok)
        def _():
            copy.start()

    def follow(before, entry):
        @pl.when(below)
        def _():
            before[0].wait_send()
            entry[0].start()

    small[0].wait()
    small[1].wait()
    widths = jnp.transpose(jnp.concatenate([widths_v[0], widths_v[1]], axis=0))
    bounds = jnp.transpose(jnp.concatenate([range_v[r, c] for r in range(2) for c in range(4)], axis=0))
    position = lax.broadcasted_iota(jnp.int32, (FPC, NPIX), 1)
    wave = lax.broadcasted_iota(jnp.int32, (1, MODES), 1).astype(F32) * (2.0 * np.pi / NPIX)

    def spectra(cells):
        windows = []
        for h, cell in enumerate(cells):
            flux_loads[cell].wait()
            low, high = bounds[:, 2 * cell:2 * cell + 1], bounds[:, 2 * cell + 1:2 * cell + 2]
            inside = (position >= low) & (position < high)
            masked[pl.ds(h * FPC, FPC)] = jnp.where(inside, flux[cell].astype(F32), 0.0).astype(BF16)
            windows.append(jnp.exp(-0.5 * (wave * widths[:, cell:cell + 1]) ** 2))
        if cells[0] == 0:
            basis_load.wait()
        for n in range(NPIX // TILE):
            cols = pl.ds(n * TILE, TILE)
            raw = jnp.dot(masked[...], basis[:, cols], preferred_element_type=F32)
            first = n * TILE % MODES
            for h, cell in enumerate(cells):
                value = raw[h * FPC:(h + 1) * FPC] * windows[h][:, first:first + TILE]
                spec[at(cell // 4, cell % 4), :, cols] = value.astype(BF16)

    spectra((0, 3))
    pl.semaphore_wait(barrier, expected)
    for entry in (down[0], down_left, side_low):
        start(entry)
    spectra((1, 2))
    spectra((4, 7))
    start(side_high)
    start(side_right)

    small[2].wait()
    ra_step, dec_step = pairs_v[0, 1], pairs_v[0, 2]
    code = pairs_v[0, 0] * 5 + jnp.where(ra_step == 0, dec_step, dec_step + 3)
    slots = code.shape[1]
    hit = code == lax.broadcasted_iota(jnp.int32, (slots, slots), 0)
    slot_id = lax.broadcasted_iota(jnp.int32, (slots, slots), 1)
    inverse = jnp.max(jnp.where(hit, slot_id, 0), axis=1, keepdims=True)
    inv_v[...] = jnp.broadcast_to(inverse, inv_v.shape)
    to_smem.start()
    live_count = count[0, 0]

    blank = jnp.zeros((FPC, NPIX), BF16)
    for gone, cells in (
        (jnp.logical_not(above), [at(2, c) for c in range(5)]),
        (jnp.logical_not(above) | even, [at(2, -1)]),
        (even, [at(1, -1)]),
        (jnp.logical_not(right), [at(0, 4), at(1, 4)]),
        (jnp.logical_not(right) & above, [at(2, 4)]),
    ):
        @pl.when(gone)
        def _():
            for cell in cells:
                spec[cell] = blank
    acc[...] = jnp.zeros_like(acc)
    cacc[...] = jnp.zeros_like(cacc)

    spectra((5, 6))
    to_smem.wait()
    sep_load.wait()

    def code_of(row, col, offset):
        return (row * 4 + col) * 5 + offset

    def bins_of(code):
        slot = inv_s[code, 0]
        return (sep[slot] + jnp.where(slot < live_count, 0, 16)).astype(F32).astype(BF16)

    @pl.when(lend_bins[1])
    def _():
        ship[0] = bins_of(code_of(0, 0, 2))
        ship[1] = bins_of(code_of(1, 0, 2))
        lend_bins[0].start()

    def spread(which, k, counted):
        for t in range(NSEP):
            ones = jnp.where(which == jnp.asarray(t, BF16), jnp.asarray(1, BF16), jnp.asarray(0, BF16))
            onehot[pl.ds(t * FPC, FPC), pl.ds(k * FPC, FPC)] = ones
            if counted:
                cacc[t] += jnp.sum(ones.astype(F32).reshape(16, 8, FPC), axis=0)

    def multiply(a, b, n, acc):
        for m in range(NPIX // TILE):
            cols = pl.ds(m * TILE, TILE)
            partner = spec[pl.ds(b, n), :, cols].reshape(n * FPC, TILE)
            own = spec[a, :, cols].astype(F32).reshape(1, 16, 8, TILE)
            mixed = jnp.dot(onehot[:, :n * FPC], partner, preferred_element_type=F32)
            acc[:, :, cols] += jnp.sum(mixed.reshape(NSEP, 16, 8, TILE) * own, axis=1)

    def pair_up(a, b, first_code, n):
        for k in range(n):
            spread(bins_of(first_code + k), k, True)
        multiply(a, b, n, acc)

    column = lax.broadcasted_iota(jnp.int32, (NPIX, NKB), 0) % MODES
    in_bin = column // (MODES // NKB) == lax.broadcasted_iota(jnp.int32, (NPIX, NKB), 1)
    table = jnp.where(in_bin, 1.0, 0.0).astype(BF16)

    def fold(acc):
        rest = acc[...].reshape(NSEP * 8, NPIX)
        folded = jnp.zeros((NSEP * 8, NKB), F32)
        for _ in range(3):
            part = rest.astype(BF16)
            folded += jnp.dot(part, table, preferred_element_type=F32)
            rest = rest - part.astype(F32)
        return jnp.sum(folded.reshape(NSEP, 8, NKB), axis=1)

    @pl.loop(0, 6)
    def _(k):
        row, col = k // 3, k % 3
        pair_up(at(row, col), at(row, col), code_of(row, col, 0), 2)

    follow(down[0], down[3])
    arrived(at(2, 0), above)
    for entry in (pass_up, pass_left):
        start(entry)

    @pl.loop(1, 3)
    def _(col):
        pair_up(at(0, col), at(1, col - 1), code_of(0, col, 2), 3)

    @pl.loop(0, 2)
    def _(k):
        col = 3 * k
        pair_up(at(0, col), at(1, col - k), code_of(0, col, 3 - k), 2)

    follow(down[3], down[1])
    arrived(at(2, 3), above)
    start(pass_right)
    arrived(at(1, 4), right)
    arrived(at(0, 4), right)

    @pl.when(give_back[1])
    def _():
        lend_bins[0].wait_recv()
        acc2[...] = jnp.zeros_like(acc2)

        @pl.loop(0, 2)
        def _(k):
            spread(shipped[k], 0, False)
            multiply(at(k, 4), at(k + 1, 3), 1, acc2)

        lent[...] = fold(acc2)
        give_back[0].start()

    @pl.loop(0, 2)
    def _(row):
        pair_up(at(row, 3), at(row, 3), code_of(row, 3, 0), 2)

    arrived(at(1, -1), odd)

    @pl.loop(0, 2)
    def _(k):
        col = 3 * k
        pair_up(at(0, col), at(1, col - 1 + 2 * k), code_of(0, col, 2 + 2 * k), 1)

    arrived(at(2, -1), above & odd)
    arrived(at(2, 4), above & right)

    @pl.loop(0, 2)
    def _(k):
        pair_up(at(1, 3 * k), at(2, 4 * k - 1), code_of(1, 3 * k, 2 + k), 2)

    follow(down[1], down[2])
    arrived(at(2, 1), above)

    @pl.loop(0, 2)
    def _(k):
        pair_up(at(1, 2 * k), at(2, 2 * k + 1), code_of(1, 2 * k, 4), 1)

    pair_up(at(1, 1), at(2, 0), code_of(1, 1, 2), 2)
    arrived(at(2, 2), above)
    pair_up(at(1, 2), at(2, 1), code_of(1, 2, 2), 2)

    @pl.loop(0, 2)
    def _(k):
        pair_up(at(1, 2 * k + 1), at(2, 2), code_of(1, 2 * k + 1, 4 - 2 * k), 1)

    pay[0] = fold(acc)

    @pl.when(lend_bins[1])
    def _():
        give_back[0].wait_recv()
        pay[0] += lent_in[...]

    pay[1] = jnp.sum(cacc[...], axis=1)

    def everyone(source, box, mine, size, sent, got, peer):
        box[mine] = source[...]

        def copy(k):
            return pltpu.make_async_remote_copy(
                src_ref=source, dst_ref=box.at[mine], send_sem=sent.at[k], recv_sem=got.at[mine],
                device_id=peer(lax.rem(mine + k, size)), device_id_type=MESH)

        for k in range(1, size):
            copy(k).start()
        for k in range(1, size):
            other = lax.rem(mine + k, size)
            pltpu.make_async_remote_copy(
                src_ref=source, dst_ref=box.at[other], send_sem=sent.at[k], recv_sem=got.at[other],
                device_id=peer(other), device_id_type=MESH).wait_recv()
        total = box[0]
        for k in range(1, size):
            total = total + box[k]
        return total, [copy(k) for k in range(1, size)]

    total, first = everyone(pay, box1, q, n_dec, sent1, got1, lambda k: (p, k))
    pay2[...] = total
    total, second = everyone(pay2, box2, p, n_ra, sent2, got2, lambda k: (k, q))
    counts = jnp.sum(total[1], axis=1, keepdims=True)
    out[0] = pay[0]
    out[1] = total[0] / jnp.maximum(counts, 1.0)

    for copy in first + second:
        copy.wait_send()
    for copy, ok in [
        down[2], down_left, side_low, side_high, side_right, pass_left, pass_right, pass_up, lend_bins, give_back
    ]:
        @pl.when(ok)
        def _():
            copy.wait_send()


def per_device(n_ra, n_dec, forests, resolution, pixel_range, pairs, count, sep):
    vmem = pl.BlockSpec(memory_space=pltpu.VMEM)
    smem = pl.BlockSpec(memory_space=pltpu.SMEM)
    anywhere = pl.BlockSpec(memory_space=pl.ANY)
    dma = pltpu.SemaphoreType.DMA
    slots = pairs.shape[2]
    pairs = jnp.transpose(pairs, (0, 3, 1, 2))
    both = pl.pallas_call(
        functools.partial(kernel, n_ra, n_dec),
        out_shape=jax.ShapeDtypeStruct((2, NSEP, NKB), F32),
        in_specs=[anywhere, anywhere, anywhere, anywhere, smem, anywhere, anywhere],
        out_specs=vmem,
        scratch_shapes=[
            pltpu.VMEM((8, FPC, NPIX), BF16),
            pltpu.VMEM((NPIX, NPIX), BF16),
            pltpu.VMEM(sep.shape[2:], jnp.int32),
            pltpu.VMEM((3 * STRIDE, FPC, NPIX), BF16),
            pltpu.VMEM((2 * FPC, NPIX), BF16),
            pltpu.VMEM((NSEP * FPC, 3 * FPC), BF16),
            pltpu.VMEM((NSEP, 8, NPIX), F32),
            pltpu.VMEM((NSEP, 8, NPIX), F32),
            pltpu.VMEM((NSEP, 8, FPC), F32),
            pltpu.VMEM((slots, 128), jnp.int32),
            pltpu.SMEM((slots, 128), jnp.int32),
            pltpu.VMEM((2, FPC, FPC), BF16),
            pltpu.VMEM((2, FPC, FPC), BF16),
            pltpu.VMEM((NSEP, NKB), F32),
            pltpu.VMEM((NSEP, NKB), F32),
            pltpu.VMEM((2, NSEP, NKB), F32),
            pltpu.VMEM((2, NSEP, NKB), F32),
            pltpu.VMEM((n_dec, 2, NSEP, NKB), F32),
            pltpu.VMEM((n_ra, 2, NSEP, NKB), F32),
            pltpu.VMEM(resolution.shape, F32),
            pltpu.VMEM(pixel_range.shape, jnp.int32),
            pltpu.VMEM(pairs.shape, jnp.int32),
            dma((14,)),
            dma((3 * STRIDE + 2,)),
            dma((13,)),
            dma((n_dec,)),
            dma((n_dec,)),
            dma((n_ra,)),
            dma((n_ra,)),
        ],
        compiler_params=pltpu.CompilerParams(
            collective_id=0, has_side_effects=True, vmem_limit_bytes=56 * 1024 * 1024
        ),
        cost_estimate=pl.CostEstimate(flops=13_000_000_000, bytes_accessed=7_000_000, transcendentals=500_000),
    )(forests, resolution, pixel_range, pairs, count, sep, jnp.asarray(dft_table()))
    return (both[0] * (1.0 / (FPC * NPIX))).reshape(1, 1, NSEP, NKB), both[1]


def solution(mesh):
    n_ra, n_dec = mesh.shape["ra"], mesh.shape["dec"]
    return jax.shard_map(
        functools.partial(per_device, n_ra, n_dec),
        mesh=mesh,
        in_specs=(
            P("ra", "dec", None, None),
            P("ra", "dec", None),
            P("ra", "dec", None, None),
            P("ra", "dec", None, None),
            P("ra", "dec"),
            P("ra", "dec", None, None, None),
        ),
        out_specs=(P("ra", "dec", None, None), P()),
        check_vma=False,
    )
```

time: 70.9 us -> 56.3 us (0.79)
  Pallas kernels: 65.4 us -> 53.5 us
  local copies, waits for them, and re-layouts: 3.91 us -> 0 us
  other arithmetic: 0 us -> 1.28 us
    pallas_call x1, Pallas kernels: 65.4 us -> 53.5 us  [per_device(): pl.pallas_call(functools.partial(kernel, n_ra, n_dec), out_shape=jax.Shap...]
    unnamed x3 -> x0, local copies, waits for them, and re-layouts: 3.91 us -> none
    squeeze x0 -> x1, other arithmetic: none -> 1.28 us  [per_device(): return ((both[0] * (1.0 / (FPC * NPIX))).reshape(1, 1, NSEP, NKB), both[1])]
where the time goes in v2:
time: 56.3 us; the launch traced here: 56.1 us
  Pallas kernels  53.5 us (95%)
  between operations  1.29 us (2%)
  other arithmetic  1.28 us (2%)
    pallas_call x1, Pallas kernels, per_device(): pl.pallas_call(functools.partial(kernel, n_ra, n_dec), out_shape=jax.Shap...  53.5 us
    squeeze x1, other arithmetic, per_device(): return ((both[0] * (1.0 / (FPC * NPIX))).reshape(1, 1, NSEP, NKB), both[1])  1.28 us

profile of v2, /device:TPU:1, one launch (start us, length us, event | category | flops | bytes accessed | tf_op | source)
XLA Modules:
  0.0 56.1 jit_solution(375940902157446422)
XLA Ops:
  1.3 53.5 %shard_map.86 = f32[2,8,128]{2,1,0:T(8,128)} custom-call(bf16[2,4,128,1024]{3,2,1,0:T(8,128)(2,1)} %forests.1, f32[2,4,128]{2,1,0:T(4,128)} %resolution.1, s32[2,4,2,128]{3,2,1,0:T(2,128)} %pixel_range.1, s32[1,3,1,40]{3,2,1,0:T(1,128)} %bitcast.5, s32[1,1]{1,0:T(1,128)S(6)} %copy.9.count, s32[1,1,40,128,128]{4,3,2,1,0:T(8,128)} %sep_hbm.1, ...), custom_call_target="tpu_custom_call" | custom-call | flops 12999999488 | bytes 7000000 | tf_op jit(solution)/shard_map/pallas_call | solution.py:354
  54.8 1.3 %slice_bitcast_fusion = (f32[8,128]{1,0:T(8,128)}, f32[1,1,8,128]{3,2,1,0:T(8,128)}) fusion(f32[2,8,128]{2,1,0:T(8,128)} %shard_map.86), kind=kLoop, calls=%fused_computation | loop fusion | flops 1024 | bytes 16384 | tf_op jit(solution)/shard_map/squeeze | solution.py:395

commit v3 on v2

--- a/solution.py
+++ b/solution.py
@@ -37,7 +37,7 @@
     n_ra, n_dec,
     forests, resolution, pixel_range, pairs, count, sep_hbm, basis_hbm,
     out,
-    flux, basis, sep, spec, masked, onehot, acc, acc2, cacc, inv_v, inv_s, ship, shipped, lent, lent_in,
+    flux, basis, sep, spec, masked, onehot, onehot2, acc, acc2, cacc, inv_v, inv_s, ship, shipped, lent, lent_in,
     pay, pay2, box1, box2, widths_v, range_v, pairs_v,
     load_sem, halo_sem, send_sem, sent1, got1, sent2, got2,
 ):
@@ -76,6 +76,9 @@
     for k in range(1, n_dec):
         pl.semaphore_signal(barrier, inc=1, device_id=(p, lax.rem(q + k, n_dec)), device_id_type=MESH)
 
+    bins_there = 3 * STRIDE
+    sums_back = bins_there + 1
+
     def send(source, target, sem, dp, dq):
         return pltpu.make_async_remote_copy(
             src_ref=spec.at[source], dst_ref=spec.at[target],
@@ -87,10 +90,20 @@
         def _():
             send(target, target, 0, 0, 0).wait_recv()
 
-    bins_there = 3 * STRIDE
-    sums_back = bins_there + 1
-    down = [(send(at(0, c), at(2, c), c, -1, 0), below) for c in range(4)]
-    down_left = (send(at(0, 0), at(2, 4), 4, -1, -1), below & left & even)
+    down = {c: (send(at(0, c), at(2, c), c, -1, 0), below) for c in (0, 1, 3)}
+
+    def half(h):
+        cols = pl.ds(h * MODES, MODES)
+        return pltpu.make_async_remote_copy(
+            src_ref=spec.at[at(0, 2), :, cols], dst_ref=spec.at[at(2, 2), :, cols],
+            send_sem=send_sem.at[15 + h], recv_sem=halo_sem.at[bins_there + 2 + h],
+            device_id=(p - 1, q), device_id_type=MESH)
+
+    last = [(half(h), below) for h in range(2)]
+    p_even = lax.rem(p, 2) == 0
+    down_left = (send(at(0, 0), at(2, 4), 4, -1, -1), left & even & jnp.logical_not(p_even))
+    to_relay = (send(at(0, 0), at(0, -1), 13, -2, 0), left & even & p_even & (p >= 2))
+    relay = (send(at(0, -1), at(2, 4), 14, 1, -1), left & even & p_even & (p + 2 < n_ra))
     side_low = (send(at(0, 0), at(0, 4), 5, 0, -1), odd | (left & jnp.logical_not(below)))
     side_high = (send(at(1, 0), at(1, 4), 6, 0, -1), left)
     side_right = (send(at(1, 3), at(1, -1), 7, 0, 1), even)
@@ -144,7 +157,7 @@
 
     spectra((0, 3))
     pl.semaphore_wait(barrier, expected)
-    for entry in (down[0], down_left, side_low):
+    for entry in (down[0], down_left, to_relay, side_low):
         start(entry)
     spectra((1, 2))
     spectra((4, 7))
@@ -194,7 +207,7 @@
         ship[1] = bins_of(code_of(1, 0, 2))
         lend_bins[0].start()
 
-    def spread(which, k, counted):
+    def spread(which, k, counted, onehot):
         for t in range(NSEP):
             ones = jnp.where(which == jnp.asarray(t, BF16), jnp.asarray(1, BF16), jnp.asarray(0, BF16))
             onehot[pl.ds(t * FPC, FPC), pl.ds(k * FPC, FPC)] = ones
@@ -211,7 +224,7 @@
 
     def pair_up(a, b, first_code, n):
         for k in range(n):
-            spread(bins_of(first_code + k), k, True)
+            spread(bins_of(first_code + k), k, True, onehot)
         multiply(a, b, n, acc)
 
     column = lax.broadcasted_iota(jnp.int32, (NPIX, NKB), 0) % MODES
@@ -233,6 +246,8 @@
         pair_up(at(row, col), at(row, col), code_of(row, col, 0), 2)
 
     follow(down[0], down[3])
+    arrived(at(0, -1), relay[1])
+    start(relay)
     arrived(at(2, 0), above)
     for entry in (pass_up, pass_left):
         start(entry)
@@ -259,7 +274,7 @@
 
         @pl.loop(0, 2)
         def _(k):
-            spread(shipped[k], 0, False)
+            spread(shipped[k], 0, False, onehot)
             multiply(at(k, 4), at(k + 1, 3), 1, acc2)
 
         lent[...] = fold(acc2)
@@ -283,7 +298,7 @@
     def _(k):
         pair_up(at(1, 3 * k), at(2, 4 * k - 1), code_of(1, 3 * k, 2 + k), 2)
 
-    follow(down[1], down[2])
+    follow(down[1], last[0])
     arrived(at(2, 1), above)
 
     @pl.loop(0, 2)
@@ -291,12 +306,26 @@
         pair_up(at(1, 2 * k), at(2, 2 * k + 1), code_of(1, 2 * k, 4), 1)
 
     pair_up(at(1, 1), at(2, 0), code_of(1, 1, 2), 2)
-    arrived(at(2, 2), above)
-    pair_up(at(1, 2), at(2, 1), code_of(1, 2, 2), 2)
-
-    @pl.loop(0, 2)
-    def _(k):
-        pair_up(at(1, 2 * k + 1), at(2, 2), code_of(1, 2 * k + 1, 4 - 2 * k), 1)
+    follow(last[0], last[1])
+
+    for k, (col, offset) in enumerate(((2, 2), (2, 3), (1, 4), (3, 2))):
+        spread(bins_of(code_of(1, col, offset)), k, True, onehot2)
+    for h in range(2):
+        @pl.when(above)
+        def _():
+            last[h][0].wait_recv()
+
+        @pl.loop(0, MODES // TILE)
+        def _(m):
+            cols = pl.ds(pl.multiple_of(h * MODES + m * TILE, TILE), TILE)
+            total = acc[:, :, cols]
+            for col, b, n, lane in ((2, 1, 2, 0), (1, 2, 1, 2), (3, 2, 1, 3)):
+                partner = spec[pl.ds(at(2, b), n), :, cols].reshape(n * FPC, TILE)
+                own = spec[at(1, col), :, cols].astype(F32).reshape(1, 16, 8, TILE)
+                ones = onehot2[:, lane * FPC:(lane + n) * FPC]
+                mixed = jnp.dot(ones, partner, preferred_element_type=F32)
+                total += jnp.sum(mixed.reshape(NSEP, 16, 8, TILE) * own, axis=1)
+            acc[:, :, cols] = total
 
     pay[0] = fold(acc)
 
@@ -315,7 +344,7 @@
                 src_ref=source, dst_ref=box.at[mine], send_sem=sent.at[k], recv_sem=got.at[mine],
                 device_id=peer(lax.rem(mine + k, size)), device_id_type=MESH)
 
-        for k in range(1, size):
+        for k in sorted(range(1, size), key=lambda k: abs(2 * k - size)):
             copy(k).start()
         for k in range(1, size):
             other = lax.rem(mine + k, size)
@@ -337,7 +366,7 @@
     for copy in first + second:
         copy.wait_send()
     for copy, ok in [
-        down[2], down_left, side_low, side_high, side_right, pass_left, pass_right, pass_up, lend_bins, give_back
+        last[1], to_relay, relay, down_left, side_low, side_high, side_right, pass_left, pass_right, pass_up, lend_bins, give_back
     ]:
         @pl.when(ok)
         def _():
@@ -363,6 +392,7 @@
             pltpu.VMEM((3 * STRIDE, FPC, NPIX), BF16),
             pltpu.VMEM((2 * FPC, NPIX), BF16),
             pltpu.VMEM((NSEP * FPC, 3 * FPC), BF16),
+            pltpu.VMEM((NSEP * FPC, 4 * FPC), BF16),
             pltpu.VMEM((NSEP, 8, NPIX), F32),
             pltpu.VMEM((NSEP, 8, NPIX), F32),
             pltpu.VMEM((NSEP, 8, FPC), F32),
@@ -380,8 +410,8 @@
             pltpu.VMEM(pixel_range.shape, jnp.int32),
             pltpu.VMEM(pairs.shape, jnp.int32),
             dma((14,)),
-            dma((3 * STRIDE + 2,)),
-            dma((13,)),
+            dma((3 * STRIDE + 4,)),
+            dma((17,)),
             dma((n_dec,)),
             dma((n_dec,)),
             dma((n_ra,)),

time: 56.3 us -> 52.5 us (0.933)
  Pallas kernels: 53.5 us -> 49.7 us
    pallas_call x1, Pallas kernels: 53.5 us -> 49.7 us  [per_device(): pl.pallas_call(functools.partial(kernel, n_ra, n_dec), out_shape=jax.Shap...]
where the time goes in v3:
time: 52.5 us; the launch traced here: 52.2 us
  Pallas kernels  49.7 us (95%)
  between operations  1.29 us (2%)
  other arithmetic  1.28 us (2%)
    pallas_call x1, Pallas kernels, per_device(): pl.pallas_call(functools.partial(kernel, n_ra, n_dec), out_shape=jax.Shap...  49.7 us
    squeeze x1, other arithmetic, per_device(): return ((both[0] * (1.0 / (FPC * NPIX))).reshape(1, 1, NSEP, NKB), both[1])  1.28 us

profile of v3, /device:TPU:1, one launch (start us, length us, event | category | flops | bytes accessed | tf_op | source)
XLA Modules:
  0.0 52.2 jit_solution(3390718978861449814)
XLA Ops:
  1.3 49.7 %shard_map.86 = f32[2,8,128]{2,1,0:T(8,128)} custom-call(bf16[2,4,128,1024]{3,2,1,0:T(8,128)(2,1)} %forests.1, f32[2,4,128]{2,1,0:T(4,128)} %resolution.1, s32[2,4,2,128]{3,2,1,0:T(2,128)} %pixel_range.1, s32[1,3,1,40]{3,2,1,0:T(1,128)} %bitcast.5, s32[1,1]{1,0:T(1,128)S(6)} %copy.9.count, s32[1,1,40,128,128]{4,3,2,1,0:T(8,128)} %sep_hbm.1, ...), custom_call_target="tpu_custom_call" | custom-call | flops 12999999488 | bytes 7000000 | tf_op jit(solution)/shard_map/pallas_call | solution.py:383
  51.0 1.3 %slice_bitcast_fusion = (f32[8,128]{1,0:T(8,128)}, f32[1,1,8,128]{3,2,1,0:T(8,128)}) fusion(f32[2,8,128]{2,1,0:T(8,128)} %shard_map.86), kind=kLoop, calls=%fused_computation | loop fusion | flops 1024 | bytes 16384 | tf_op jit(solution)/shard_map/squeeze | solution.py:425

commit v4 on v3

--- a/solution.py
+++ b/solution.py
@@ -149,18 +149,18 @@
             basis_load.wait()
         for n in range(NPIX // TILE):
             cols = pl.ds(n * TILE, TILE)
-            raw = jnp.dot(masked[...], basis[:, cols], preferred_element_type=F32)
+            raw = jnp.dot(masked[:len(cells) * FPC], basis[:, cols], preferred_element_type=F32)
             first = n * TILE % MODES
             for h, cell in enumerate(cells):
                 value = raw[h * FPC:(h + 1) * FPC] * windows[h][:, first:first + TILE]
                 spec[at(cell // 4, cell % 4), :, cols] = value.astype(BF16)
 
-    spectra((0, 3))
+    spectra((0,))
     pl.semaphore_wait(barrier, expected)
     for entry in (down[0], down_left, to_relay, side_low):
         start(entry)
-    spectra((1, 2))
-    spectra((4, 7))
+    spectra((3, 1))
+    spectra((2, 4, 7))
     start(side_high)
     start(side_right)
 
@@ -299,6 +299,7 @@
         pair_up(at(1, 3 * k), at(2, 4 * k - 1), code_of(1, 3 * k, 2 + k), 2)
 
     follow(down[1], last[0])
+    start(last[1])
     arrived(at(2, 1), above)
 
     @pl.loop(0, 2)
@@ -306,7 +307,6 @@
         pair_up(at(1, 2 * k), at(2, 2 * k + 1), code_of(1, 2 * k, 4), 1)
 
     pair_up(at(1, 1), at(2, 0), code_of(1, 1, 2), 2)
-    follow(last[0], last[1])
 
     for k, (col, offset) in enumerate(((2, 2), (2, 3), (1, 4), (3, 2))):
         spread(bins_of(code_of(1, col, offset)), k, True, onehot2)
@@ -366,7 +366,7 @@
     for copy in first + second:
         copy.wait_send()
     for copy, ok in [
-        last[1], to_relay, relay, down_left, side_low, side_high, side_right, pass_left, pass_right, pass_up, lend_bins, give_back
+        last[0], last[1], to_relay, relay, down_left, side_low, side_high, side_right, pass_left, pass_right, pass_up, lend_bins, give_back
     ]:
         @pl.when(ok)
         def _():
@@ -390,7 +390,7 @@
             pltpu.VMEM((NPIX, NPIX), BF16),
             pltpu.VMEM(sep.shape[2:], jnp.int32),
             pltpu.VMEM((3 * STRIDE, FPC, NPIX), BF16),
-            pltpu.VMEM((2 * FPC, NPIX), BF16),
+            pltpu.VMEM((3 * FPC, NPIX), BF16),
             pltpu.VMEM((NSEP * FPC, 3 * FPC), BF16),
             pltpu.VMEM((NSEP * FPC, 4 * FPC), BF16),
             pltpu.VMEM((NSEP, 8, NPIX), F32),

time: 52.5 us -> 51.5 us (0.981)
  Pallas kernels: 49.7 us -> 48.8 us
    pallas_call x1, Pallas kernels: 49.7 us -> 48.8 us  [per_device(): pl.pallas_call(functools.partial(kernel, n_ra, n_dec), out_shape=jax.Shap...]
where the time goes in v4:
time: 51.5 us; the launch traced here: 51.3 us
  Pallas kernels  48.8 us (95%)
  between operations  1.29 us (3%)
  other arithmetic  1.28 us (2%)
    pallas_call x1, Pallas kernels, per_device(): pl.pallas_call(functools.partial(kernel, n_ra, n_dec), out_shape=jax.Shap...  48.8 us
    squeeze x1, other arithmetic, per_device(): return ((both[0] * (1.0 / (FPC * NPIX))).reshape(1, 1, NSEP, NKB), both[1])  1.28 us

profile of v4, /device:TPU:1, one launch (start us, length us, event | category | flops | bytes accessed | tf_op | source)
XLA Modules:
  0.0 51.3 jit_solution(727931949348934699)
XLA Ops:
  1.3 48.8 %shard_map.86 = f32[2,8,128]{2,1,0:T(8,128)} custom-call(bf16[2,4,128,1024]{3,2,1,0:T(8,128)(2,1)} %forests.1, f32[2,4,128]{2,1,0:T(4,128)} %resolution.1, s32[2,4,2,128]{3,2,1,0:T(2,128)} %pixel_range.1, s32[1,3,1,40]{3,2,1,0:T(1,128)} %bitcast.5, s32[1,1]{1,0:T(1,128)S(6)} %copy.9.count, s32[1,1,40,128,128]{4,3,2,1,0:T(8,128)} %sep_hbm.1, ...), custom_call_target="tpu_custom_call" | custom-call | flops 12999999488 | bytes 7000000 | tf_op jit(solution)/shard_map/pallas_call | solution.py:383
  50.0 1.3 %slice_bitcast_fusion = (f32[8,128]{1,0:T(8,128)}, f32[1,1,8,128]{3,2,1,0:T(8,128)}) fusion(f32[2,8,128]{2,1,0:T(8,128)} %shard_map.86), kind=kLoop, calls=%fused_computation | loop fusion | flops 1024 | bytes 16384 | tf_op jit(solution)/shard_map/squeeze | solution.py:425
